TPU v7x, 512 devices: a whole 4x4x16 slice. The times are simulated.
512 devices in a mesh: layer: 8 (over z_hi, x), row: 8 (over z_lo), col: 8 (over y, core).
Axes of the slice: x: 4, y: 4, z: 16 (z_hi: 2, z_lo: 8; z = z_hi * 8 + z_lo), core: 2. Of those that a mesh axis runs over, the one named last changes fastest.
Arguments:
- covariance: float32 [65536, 8192], P(('layer', 'row'), 'col'), parts along dimension 0, may hold values from -2 to 20, as said below
- weight: bfloat16 [65536, 2, 1024], P(('layer', 'col', 'row')), parts along dimension 0, may hold values from -6 to 6
- factor_a: bfloat16 [65536, 2, 256], P(('layer', 'col', 'row')), parts along dimension 0, may hold values from -1.5 to 1.5
- factor_b: bfloat16 [16, 256, 1024], P('layer', ('row', 'col')), parts along dimension 0, may hold values from -1.5 to 1.5
Outputs:
- new_a: float32 [65536, 2, 256], P(('layer', 'col', 'row')), parts along dimension 0
- new_b: float32 [16, 256, 1024], P('layer', ('row', 'col')), parts along dimension 0
There are 8 independent parts, one for each index of `layer`. A program takes and returns all parts, laid end to end along the dimension named above; each array names one. Nothing has to cross between parts.
Inputs may be any that keep to these rules, and one draw needn't show every extreme that they name: covariance is symmetric and positive definite.
All inputs are finite; a program needn't handle non-finite values.
Results may differ from a plain program's by a relative error of at most 0.0012.
Values may be sent and summed in bfloat16 or wider, within the bound.
A program may use at most 64 MiB of HBM per device.

v0:
```python
import jax
import jax.numpy as jnp
from jax import lax
from jax.sharding import PartitionSpec as P

D = 8192
O = 1024
R = 256


def reorder_slots(spread):
    side = lax.axis_size("row")
    total = side * side
    return spread.reshape(side, side, -1).transpose(1, 0, 2).reshape(total, -1)


def transpose_full(values):
    side = lax.axis_size("row")
    flat = values.reshape(side * side, -1)
    spread = lax.all_to_all(flat, ("row", "col"), split_axis=0, concat_axis=0, tiled=True)
    landed = lax.all_to_all(
        reorder_slots(spread), ("row", "col"), split_axis=0, concat_axis=0, tiled=True
    )
    return landed.reshape(values.shape)


def per_device(covariance, weight, factor_a, factor_b):
    highest = lax.Precision.HIGHEST
    row_count = weight.shape[0]
    full_b = lax.all_gather(factor_b, ("row", "col"), axis=1, tiled=True)
    right_f = full_b.astype(jnp.float32)
    diff_one = (
        weight.astype(jnp.float32)
        - jnp.einsum("nkr,kro->nko", factor_a, full_b, preferred_element_type=jnp.float32)
    ).astype(jnp.bfloat16)
    panels = jnp.einsum(
        "nko,kro->nkr",
        lax.all_gather(diff_one, "row", axis=0, tiled=True),
        full_b,
        preferred_element_type=jnp.float32,
    )
    panel_flat = panels.reshape(panels.shape[0], -1)
    cov_rows = covariance
    grad_one = lax.psum_scatter(
        jnp.dot(cov_rows, panel_flat, precision=highest, preferred_element_type=jnp.float32),
        "col",
        scatter_dimension=0,
        tiled=True,
    )
    grad_one = transpose_full(grad_one)
    new_a = factor_a.astype(jnp.float32) + 4.0 / O * grad_one.reshape(row_count, 2, R)
    diff_two = (
        weight.astype(jnp.float32) - jnp.einsum("nkr,kro->nko", new_a, right_f, precision=highest)
    ).astype(jnp.bfloat16)
    a_panel = lax.all_gather(new_a.reshape(row_count, 2 * R), "row", axis=0, tiled=True)
    cov_rows = covariance
    field = lax.psum_scatter(
        jnp.dot(cov_rows, a_panel, precision=highest, preferred_element_type=jnp.float32),
        "col",
        scatter_dimension=0,
        tiled=True,
    )
    field = transpose_full(field)
    partial_value = jnp.einsum(
        "nkr,nko->kro",
        field.reshape(row_count, 2, R),
        diff_two.astype(jnp.float32),
        precision=highest,
    )
    summed = lax.psum(partial_value, ("row", "col"))
    share_rows = factor_b.shape[1]
    linear_id = lax.axis_index("row") * lax.axis_size("col") + lax.axis_index("col")
    own_share = lax.dynamic_slice_in_dim(summed, linear_id * share_rows, share_rows, 1)
    new_b = factor_b.astype(jnp.float32) + 8.0 / D * own_share
    return (new_a, new_b)


def solution(mesh):
    in_specs = (
        P(("layer", "row"), "col"),
        P(("layer", "col", "row"), None, None),
        P(("layer", "col", "row"), None, None),
        P("layer", ("row", "col"), None),
    )
    out_specs = (P(("layer", "col", "row"), None, None), P("layer", ("row", "col"), None))
    return jax.shard_map(
        per_device, mesh=mesh, in_specs=in_specs, out_specs=out_specs, check_vma=False
    )
```

profile of v0, /device:TPU:1, one launch (start us, length us, event | category | flops | bytes accessed | tf_op | source)
XLA Modules:
  0.0 1366.5 jit_solution(1264701732032202692)
XLA Ops:
  7.2 0.0 all-gather.4.cloned.1.call-start
  7.2 1.3 copy.42
  8.5 0.0 all-gather.4.cloned.1.call-update
  8.6 0.0 all-gather.6.cloned.1.call-start
  8.6 1.4 copy.41
  10.0 125.7 %all-gather.4.cloned.1.call-done = bf16[2,256,1024]{2,0,1:T(2,128)(2,1)} async-done(((bf16[2,4,1024]{2,0,1:T(2,128)(2,1)}), bf16[2,256,1024]{2,0,1:T(2,128)(2,1)}) %all-gather.4.cloned.1.call-update) | async-done | bytes 1048592 | tf_op jit(solution)/shard_map/all_gather | solution.py:30
  135.7 2.7 fusion.3
  138.4 0.0 all-gather.6.cloned.1.call-update
  138.4 0.0 reduce-scatter.3.cloned.1.call-start
  138.5 101.9 %all-gather.6.cloned.1.call-done = bf16[1024,2,1024]{0,2,1:T(8,128)(2,1)} async-done(((bf16[128,2,1024]{0,2,1:T(8,128)(2,1)}), bf16[1024,2,1024]{0,2,1:T(8,128)(2,1)}) %all-gather.6.cloned.1.call-update) | async-done | bytes 4194320 | tf_op jit(solution)/shard_map/all_gather | solution.py:38
  240.4 3.6 fusion.5
  244.0 8.3 convolution_bitcast_fusion.1
  252.3 0.0 reduce-scatter.3.cloned.1.call-update
  252.3 0.0 all-gather.8.cloned.1.call-start
  252.3 39.2 %reduce-scatter.3.cloned.1.call-done = f32[128,512]{0,1:T(8,128)} async-done(((f32[1024,512]{0,1:T(8,128)}), f32[128,512]{0,1:T(8,128)}) %reduce-scatter.3.cloned.1.call-update) | async-done | bytes 262160 | tf_op jit(solution)/shard_map/reduce_scatter | solution.py:44
  291.5 1.1 copy.47
  292.6 0.0 copy-start.3
  292.6 0.3 all_to_all.32
  292.9 32.7 %all_to_all.38 = f32[64,1,1024]{2,1,0:T(1,128)S(1)} all-to-all(f32[64,1,1024]{2,1,0:T(1,128)S(1)} %all_to_all.32), channel_id=1, replica_groups=mesh['layer'=8,'row'=8,'col'=8] {'row','col'}, dimensions={0} | all-to-all | bytes 524288 | tf_op jit(solution)/shard_map/all_to_all | solution.py:20
  325.7 0.2 copy.85
  325.9 0.3 copy.50
  326.1 25.6 %all_to_all.39 = f32[64,1,1024]{2,1,0:T(1,128)S(1)} all-to-all(f32[64,1,1024]{2,1,0:T(1,128)S(1)} %copy.50), channel_id=1, replica_groups=mesh['layer'=8,'row'=8,'col'=8] {'row','col'}, dimensions={0} | all-to-all | bytes 524288 | tf_op jit(solution)/shard_map/all_to_all | solution.py:21
  351.7 0.7 multiply_reduce_fusion
  352.4 0.2 mul.23
  352.7 0.0 copy-start.2
  352.7 0.8 copy.65
  353.5 0.0 all-gather.8.cloned.1.call-update
  353.5 0.0 reduce-scatter.5.cloned.1.call-start
  353.6 58.1 %all-gather.8.cloned.1.call-done = f32[1024,512]{1,0:T(8,128)} async-done(((f32[128,512]{1,0:T(8,128)}), f32[1024,512]{1,0:T(8,128)}) %all-gather.8.cloned.1.call-update) | async-done | bytes 2097168 | tf_op jit(solution)/shard_map/all_gather | solution.py:55
  411.7 16.7 %convolution_bitcast_fusion = f32[1024,512]{0,1:T(8,128)} fusion(f32[1024,512]{1,0:T(8,128)} %all-gather.8.cloned.1.call-done, f32[1024,1024]{1,0:T(8,128)} %param.4), kind=kOutput, calls=%fused_computation | convolution fusion | flops 6442450944 | bytes 8388608 | tf_op jit(solution)/shard_map/dot_general | solution.py:58
  428.4 0.0 reduce-scatter.5.cloned.1.call-update
  428.4 40.4 %reduce-scatter.5.cloned.1.call-done = f32[128,512]{0,1:T(8,128)} async-done(((f32[1024,512]{0,1:T(8,128)}), f32[128,512]{0,1:T(8,128)}) %reduce-scatter.5.cloned.1.call-update) | async-done | bytes 262160 | tf_op jit(solution)/shard_map/reduce_scatter | solution.py:57
  468.8 1.1 copy.51
  469.9 0.3 all_to_all.33
  470.2 32.8 %all_to_all.40 = f32[64,1,1024]{2,1,0:T(1,128)S(1)} all-to-all(f32[64,1,1024]{2,1,0:T(1,128)S(1)} %all_to_all.33), channel_id=1, replica_groups=mesh['layer'=8,'row'=8,'col'=8] {'row','col'}, dimensions={0} | all-to-all | bytes 524288 | tf_op jit(solution)/shard_map/all_to_all | solution.py:20
  503.1 0.2 copy.84
  503.2 1.0 copy.54
  504.2 5.9 all-to-all-start.3
  510.2 0.3 all-reduce.2.cloned.1.call-start
  510.4 1.3 fusion.2
  511.8 18.2 %all-to-all-done.3 = f32[64,1,1024]{2,1,0:T(1,128)S(1)} async-done(((f32[64,1,1024]{2,1,0:T(1,128)}), f32[64,1,1024]{2,1,0:T(1,128)S(1)}, u32[]{:S(2)}, u32[]{:S(2)}) %all-to-all-start.3) | async-done | bytes 262176 | tf_op jit(solution)/shard_map/all_to_all | solution.py:21
  530.0 0.6 reduce.1
  530.6 0.2 reshape_reshape.4
  530.8 0.0 copy-start.4
  530.9 2.4 fusion.8
  533.2 0.0 all-reduce.2.cloned.1.call-update
  533.2 825.0 %all-reduce.2.cloned.1.call-done = f32[2,256,1024]{2,1,0:T(8,128)} async-done(((f32[2,256,1024]{2,1,0:T(8,128)}), f32[2,256,1024]{2,1,0:T(8,128)}) %all-reduce.2.cloned.1.call-update) | async-done | bytes 2097168 | tf_op jit(solution)/shard_map/psum | solution.py:70
  1358.2 1.5 multiply_add_fusion
  (10 shorter events, 0.1 us)
Async XLA Ops:
  7.2 128.5 %all-gather.4.cloned.1.call-start = ((), (), s32[]{:S(2)}) async-start(), calls=%async_computation.6 | async-start | bytes 1064960 | tf_op jit(solution)/shard_map/all_gather | solution.py:30
  8.6 231.8 %all-gather.6.cloned.1.call-start = ((), (), s32[]{:S(2)}) async-start(), calls=%async_computation.7 | async-start | bytes 4718592 | tf_op jit(solution)/shard_map/all_gather | solution.py:38
  135.7 104.7 %copy-start.1 = (bf16[2,256,1024]{2,0,1:T(2,128)(2,1)S(1)}, bf16[2,256,1024]{2,0,1:T(2,128)(2,1)}, u32[]{:S(2)}) copy-start(bf16[2,256,1024]{2,0,1:T(2,128)(2,1)} %all-gather.4.cloned.1.call-done) | copy-start | bytes 3145732
  138.4 153.1 %reduce-scatter.3.cloned.1.call-start = ((), (), s32[]{:S(2)}) async-start(), calls=%async_computation.8 | async-start | bytes 2359296 | tf_op jit(solution)/shard_map/reduce_scatter | solution.py:44
  240.4 3.6 copy-start
  252.3 159.4 %all-gather.8.cloned.1.call-start = ((), (), s32[]{:S(2)}) async-start(), calls=%async_computation.9 | async-start | bytes 2359296 | tf_op jit(solution)/shard_map/all_gather | solution.py:55
  292.6 60.1 %copy-start.3 = (bf16[128,2,256]{2,1,0:T(2,128)(2,1)S(1)}, bf16[128,2,256]{2,1,0:T(2,128)(2,1)}, u32[]{:S(2)}) copy-start(bf16[128,2,256]{2,1,0:T(2,128)(2,1)} %param.6) | copy-start | bytes 393220
  352.7 157.7 %copy-start.2 = (f32[32,8,256]{2,1,0:T(8,128)}, f32[32,8,256]{2,1,0:T(8,128)S(1)}, u32[]{:S(2)}) copy-start(f32[32,8,256]{2,1,0:T(8,128)S(1)} %convert_add_fusion) | copy-start | bytes 786436
  353.5 115.2 %reduce-scatter.5.cloned.1.call-start = ((), (), s32[]{:S(2)}) async-start(), calls=%async_computation.10 | async-start | bytes 2359296 | tf_op jit(solution)/shard_map/reduce_scatter | solution.py:57
  504.2 25.8 %all-to-all-start.3 = ((f32[64,1,1024]{2,1,0:T(1,128)}), f32[64,1,1024]{2,1,0:T(1,128)S(1)}, u32[]{:S(2)}, u32[]{:S(2)}) async-start(f32[64,1,1024]{2,1,0:T(1,128)} %copy.54), calls=%async_computation.5 | async-start | bytes 524288 | tf_op jit(solution)/shard_map/all_to_all | solution.py:21
  510.2 848.1 %all-reduce.2.cloned.1.call-start = ((), (), s32[]{:S(2)}) async-start(), calls=%async_computation.11 | async-start | bytes 4194304 | tf_op jit(solution)/shard_map/psum | solution.py:70
  530.8 827.4 %copy-start.4 = (bf16[2,4,1024]{2,1,0:T(4,128)(2,1)S(1)}, bf16[2,4,1024]{2,1,0:T(4,128)(2,1)}, u32[]{:S(2)}) copy-start(bf16[2,4,1024]{2,1,0:T(4,128)(2,1)} %param.7) | copy-start | bytes 49156
Sparse Core Ops, SparseCore 0:
  10.7 124.9 all-gather.3
  138.6 101.7 all-gather.5
  252.4 39.0 reduce-scatter.2
  353.7 58.0 all-gather.7
  428.5 40.2 reduce-scatter.4
  533.4 824.8 all-reduce.1
where the time goes:
time: 1370 us
  waiting for transfers between devices  1210 us (88%)
  blocking collectives  91.1 us (7%)
  matrix products  34.9 us (3%)
  between operations  14.3 us (1%)
    psum x1, waiting for transfers between devices, per_device(): summed = lax.psum(partial_value, ('row', 'col'))  825 us
    all_gather x1, waiting for transfers between devices, per_device(): full_b = lax.all_gather(factor_b, ('row', 'col'), axis=1, tiled=True)  126 us
    all_gather x1, waiting for transfers between devices, per_device(): lax.all_gather(diff_one, 'row', axis=0, tiled=True)  102 us
    all_to_all x2, blocking collectives, transpose_full(): lax.all_to_all(flat, ('row', 'col'), split_axis=0, concat_axis=0, tiled=T...  65.6 us
    all_gather x1, waiting for transfers between devices, per_device(): lax.all_gather(new_a.reshape(row_count, 2 * R), 'row', axis=0, tiled=True)  58.1 us
    reduce_scatter x1, waiting for transfers between devices, per_device(): lax.psum_scatter(jnp.dot(cov_rows, a_panel, precision=highest, preferred_...  40.4 us
    reduce_scatter x1, waiting for transfers between devices, per_device(): lax.psum_scatter(jnp.dot(cov_rows, panel_flat, precision=highest, preferr...  39.2 us
  transfers between devices with their start and end apart: 7, of which 7 were waited for; matrix products, arithmetic and copies ran while one was open for 0% of the time, Pallas kernels for 0%

commit v1 on v0

--- a/solution.py
+++ b/solution.py
@@ -67,7 +67,7 @@
         diff_two.astype(jnp.float32),
         precision=highest,
     )
-    summed = lax.psum(partial_value, ("row", "col"))
+    summed = lax.psum(lax.psum(partial_value, "row"), "col")
     share_rows = factor_b.shape[1]
     linear_id = lax.axis_index("row") * lax.axis_size("col") + lax.axis_index("col")
     own_share = lax.dynamic_slice_in_dim(summed, linear_id * share_rows, share_rows, 1)

time: 1370 us -> 753 us (0.55)
  waiting for transfers between devices: 1210 us -> 593 us
    psum x1 -> x2, waiting for transfers between devices: 825 us -> 210 us  [per_device(): summed = lax.psum(lax.psum(partial_value, 'row'), 'col')]
  transfers between devices with their start and end apart: 7 -> 8, of which waited for: 7 -> 8; matrix products, arithmetic and copies ran while one was open for 0% -> 0% of each run, Pallas kernels for 0% -> 0%
where the time goes in v1:
time: 753 us; the launch traced here: 751 us
  waiting for transfers between devices  593 us (79%)
  blocking collectives  91.1 us (12%)
  matrix products  34.9 us (5%)
  between operations  14.3 us (2%)
  local copies, waits for them, and re-layouts  8.4 us (1%)
    psum x2, waiting for transfers between devices, per_device(): summed = lax.psum(lax.psum(partial_value, 'row'), 'col')  210 us
    all_gather x1, waiting for transfers between devices, per_device(): full_b = lax.all_gather(factor_b, ('row', 'col'), axis=1, tiled=True)  126 us
    all_gather x1, waiting for transfers between devices, per_device(): lax.all_gather(diff_one, 'row', axis=0, tiled=True)  102 us
    all_to_all x2, blocking collectives, transpose_full(): lax.all_to_all(flat, ('row', 'col'), split_axis=0, concat_axis=0, tiled=T...  65.6 us
    all_gather x1, waiting for transfers between devices, per_device(): lax.all_gather(new_a.reshape(row_count, 2 * R), 'row', axis=0, tiled=True)  58.1 us
    reduce_scatter x1, waiting for transfers between devices, per_device(): lax.psum_scatter(jnp.dot(cov_rows, a_panel, precision=highest, preferred_...  40.4 us
    reduce_scatter x1, waiting for transfers between devices, per_device(): lax.psum_scatter(jnp.dot(cov_rows, panel_flat, precision=highest, preferr...  39.2 us
    all_to_all x1, blocking collectives, transpose_full(): lax.all_to_all(reorder_slots(spread), ('row', 'col'), split_axis=0, conca...  25.6 us
  transfers between devices with their start and end apart: 8, of which 8 were waited for; matrix products, arithmetic and copies ran while one was open for 0% of the time, Pallas kernels for 0%

profile of v1, /device:TPU:1, one launch (start us, length us, event | category | flops | bytes accessed | tf_op | source)
XLA Modules:
  0.0 751.3 jit_solution(3866277768567459594)
XLA Ops:
  7.2 0.0 all-gather.4.cloned.1.call-start
  7.2 1.3 copy.42
  8.5 0.0 all-gather.4.cloned.1.call-update
  8.6 0.0 all-gather.6.cloned.1.call-start
  8.6 1.4 copy.41
  10.0 125.7 %all-gather.4.cloned.1.call-done = bf16[2,256,1024]{2,0,1:T(2,128)(2,1)} async-done(((bf16[2,4,1024]{2,0,1:T(2,128)(2,1)}), bf16[2,256,1024]{2,0,1:T(2,128)(2,1)}) %all-gather.4.cloned.1.call-update) | async-done | bytes 1048592 | tf_op jit(solution)/shard_map/all_gather | solution.py:30
  135.7 2.7 fusion.3
  138.4 0.0 all-gather.6.cloned.1.call-update
  138.4 0.0 reduce-scatter.3.cloned.1.call-start
  138.5 101.9 %all-gather.6.cloned.1.call-done = bf16[1024,2,1024]{0,2,1:T(8,128)(2,1)} async-done(((bf16[128,2,1024]{0,2,1:T(8,128)(2,1)}), bf16[1024,2,1024]{0,2,1:T(8,128)(2,1)}) %all-gather.6.cloned.1.call-update) | async-done | bytes 4194320 | tf_op jit(solution)/shard_map/all_gather | solution.py:38
  240.4 3.6 fusion.5
  244.0 8.3 %convolution_bitcast_fusion.1 = f32[1024,512]{0,1:T(8,128)} fusion(f32[1024,512]{0,1:T(8,128)S(1)} %bitcast.46, f32[1024,1024]{1,0:T(8,128)S(1)} %copy-done), kind=kOutput, calls=%fused_computation.1 | convolution fusion | flops 6442450944 | bytes 8388608 | tf_op jit(solution)/shard_map/dot_general | solution.py:45
  252.3 0.0 reduce-scatter.3.cloned.1.call-update
  252.3 0.0 all-gather.8.cloned.1.call-start
  252.3 39.2 %reduce-scatter.3.cloned.1.call-done = f32[128,512]{0,1:T(8,128)} async-done(((f32[1024,512]{0,1:T(8,128)}), f32[128,512]{0,1:T(8,128)}) %reduce-scatter.3.cloned.1.call-update) | async-done | bytes 262160 | tf_op jit(solution)/shard_map/reduce_scatter | solution.py:44
  291.5 1.1 copy.47
  292.6 0.3 all_to_all.32
  292.9 32.7 %all_to_all.38 = f32[64,1,1024]{2,1,0:T(1,128)S(1)} all-to-all(f32[64,1,1024]{2,1,0:T(1,128)S(1)} %all_to_all.32), channel_id=1, replica_groups=mesh['layer'=8,'row'=8,'col'=8] {'row','col'}, dimensions={0} | all-to-all | bytes 524288 | tf_op jit(solution)/shard_map/all_to_all | solution.py:20
  325.7 0.2 copy.85
  325.9 0.3 copy.50
  326.1 25.6 %all_to_all.39 = f32[64,1,1024]{2,1,0:T(1,128)S(1)} all-to-all(f32[64,1,1024]{2,1,0:T(1,128)S(1)} %copy.50), channel_id=1, replica_groups=mesh['layer'=8,'row'=8,'col'=8] {'row','col'}, dimensions={0} | all-to-all | bytes 524288 | tf_op jit(solution)/shard_map/all_to_all | solution.py:21
  351.7 0.7 multiply_reduce_fusion
  352.4 0.2 mul.23
  352.7 0.8 copy.65
  353.5 0.0 all-gather.8.cloned.1.call-update
  353.5 0.0 reduce-scatter.5.cloned.1.call-start
  353.6 58.1 %all-gather.8.cloned.1.call-done = f32[1024,512]{1,0:T(8,128)} async-done(((f32[128,512]{1,0:T(8,128)}), f32[1024,512]{1,0:T(8,128)}) %all-gather.8.cloned.1.call-update) | async-done | bytes 2097168 | tf_op jit(solution)/shard_map/all_gather | solution.py:55
  411.7 16.7 %convolution_bitcast_fusion = f32[1024,512]{0,1:T(8,128)} fusion(f32[1024,512]{1,0:T(8,128)} %all-gather.8.cloned.1.call-done, f32[1024,1024]{1,0:T(8,128)} %param.4), kind=kOutput, calls=%fused_computation | convolution fusion | flops 6442450944 | bytes 8388608 | tf_op jit(solution)/shard_map/dot_general | solution.py:58
  428.4 0.0 reduce-scatter.5.cloned.1.call-update
  428.4 40.4 %reduce-scatter.5.cloned.1.call-done = f32[128,512]{0,1:T(8,128)} async-done(((f32[1024,512]{0,1:T(8,128)}), f32[128,512]{0,1:T(8,128)}) %reduce-scatter.5.cloned.1.call-update) | async-done | bytes 262160 | tf_op jit(solution)/shard_map/reduce_scatter | solution.py:57
  468.8 1.1 copy.51
  469.9 0.3 all_to_all.33
  470.2 32.8 %all_to_all.40 = f32[64,1,1024]{2,1,0:T(1,128)S(1)} all-to-all(f32[64,1,1024]{2,1,0:T(1,128)S(1)} %all_to_all.33), channel_id=1, replica_groups=mesh['layer'=8,'row'=8,'col'=8] {'row','col'}, dimensions={0} | all-to-all | bytes 524288 | tf_op jit(solution)/shard_map/all_to_all | solution.py:20
  503.1 0.2 copy.84
  503.2 1.0 copy.54
  504.2 5.9 all-to-all-start.3
  510.2 0.3 all-reduce.3.cloned.1.call-start
  510.4 1.3 fusion.2
  511.8 18.2 %all-to-all-done.3 = f32[64,1,1024]{2,1,0:T(1,128)S(1)} async-done(((f32[64,1,1024]{2,1,0:T(1,128)}), f32[64,1,1024]{2,1,0:T(1,128)S(1)}, u32[]{:S(2)}, u32[]{:S(2)}) %all-to-all-start.3) | async-done | bytes 262176 | tf_op jit(solution)/shard_map/all_to_all | solution.py:21
  530.0 0.6 reduce.1
  530.6 0.2 reshape_reshape.4
  530.8 2.3 fusion.8
  533.2 0.0 all-reduce.3.cloned.1.call-update
  533.2 0.0 all-reduce.5.cloned.1.call-start
  533.3 127.8 %all-reduce.3.cloned.1.call-done = f32[2,256,1024]{2,1,0:T(8,128)} async-done(((f32[2,256,1024]{2,1,0:T(8,128)}), f32[2,256,1024]{2,1,0:T(8,128)}) %all-reduce.3.cloned.1.call-update) | async-done | bytes 2097168 | tf_op jit(solution)/shard_map/psum | solution.py:70
  661.1 0.0 all-reduce.5.cloned.1.call-update
  661.1 81.9 %all-reduce.5.cloned.1.call-done = f32[2,256,1024]{2,1,0:T(8,128)} async-done(((f32[2,256,1024]{2,1,0:T(8,128)}), f32[2,256,1024]{2,1,0:T(8,128)}) %all-reduce.5.cloned.1.call-update) | async-done | bytes 2097168 | tf_op jit(solution)/shard_map/psum | solution.py:70
  743.0 1.5 multiply_add_fusion
  (13 shorter events, 0.1 us)
Async XLA Ops:
  7.2 128.5 %all-gather.4.cloned.1.call-start = ((), (), s32[]{:S(2)}) async-start(), calls=%async_computation.6 | async-start | bytes 1064960 | tf_op jit(solution)/shard_map/all_gather | solution.py:30
  8.6 231.8 %all-gather.6.cloned.1.call-start = ((), (), s32[]{:S(2)}) async-start(), calls=%async_computation.7 | async-start | bytes 4718592 | tf_op jit(solution)/shard_map/all_gather | solution.py:38
  135.7 104.7 %copy-start.1 = (bf16[2,256,1024]{2,0,1:T(2,128)(2,1)S(1)}, bf16[2,256,1024]{2,0,1:T(2,128)(2,1)}, u32[]{:S(2)}) copy-start(bf16[2,256,1024]{2,0,1:T(2,128)(2,1)} %all-gather.4.cloned.1.call-done) | copy-start | bytes 3145732
  138.4 153.1 %reduce-scatter.3.cloned.1.call-start = ((), (), s32[]{:S(2)}) async-start(), calls=%async_computation.8 | async-start | bytes 2359296 | tf_op jit(solution)/shard_map/reduce_scatter | solution.py:44
  240.4 3.6 copy-start
  252.3 159.4 %all-gather.8.cloned.1.call-start = ((), (), s32[]{:S(2)}) async-start(), calls=%async_computation.9 | async-start | bytes 2359296 | tf_op jit(solution)/shard_map/all_gather | solution.py:55
  292.6 60.1 %copy-start.3 = (bf16[128,2,256]{2,1,0:T(2,128)(2,1)S(1)}, bf16[128,2,256]{2,1,0:T(2,128)(2,1)}, u32[]{:S(2)}) copy-start(bf16[128,2,256]{2,1,0:T(2,128)(2,1)} %param.6) | copy-start | bytes 393220
  352.7 157.7 %copy-start.2 = (f32[32,8,256]{2,1,0:T(8,128)}, f32[32,8,256]{2,1,0:T(8,128)S(1)}, u32[]{:S(2)}) copy-start(f32[32,8,256]{2,1,0:T(8,128)S(1)} %convert_add_fusion) | copy-start | bytes 786436
  353.5 115.2 %reduce-scatter.5.cloned.1.call-start = ((), (), s32[]{:S(2)}) async-start(), calls=%async_computation.10 | async-start | bytes 2359296 | tf_op jit(solution)/shard_map/reduce_scatter | solution.py:57
  504.2 25.8 %all-to-all-start.3 = ((f32[64,1,1024]{2,1,0:T(1,128)}), f32[64,1,1024]{2,1,0:T(1,128)S(1)}, u32[]{:S(2)}, u32[]{:S(2)}) async-start(f32[64,1,1024]{2,1,0:T(1,128)} %copy.54), calls=%async_computation.5 | async-start | bytes 524288 | tf_op jit(solution)/shard_map/all_to_all | solution.py:21
  510.2 150.9 %all-reduce.3.cloned.1.call-start = ((), (), s32[]{:S(2)}) async-start(), calls=%async_computation.11 | async-start | bytes 4194304 | tf_op jit(solution)/shard_map/psum | solution.py:70
  533.2 209.8 %copy-start.4 = (bf16[2,4,1024]{2,1,0:T(4,128)(2,1)S(1)}, bf16[2,4,1024]{2,1,0:T(4,128)(2,1)}, u32[]{:S(2)}) copy-start(bf16[2,4,1024]{2,1,0:T(4,128)(2,1)} %param.7) | copy-start | bytes 49156
  533.2 209.8 %all-reduce.5.cloned.1.call-start = ((), (), s32[]{:S(2)}) async-start(), calls=%async_computation.12 | async-start | bytes 4194304 | tf_op jit(solution)/shard_map/psum | solution.py:70
Sparse Core Ops, SparseCore 0:
  10.7 124.9 all-gather.3
  138.6 101.7 all-gather.5
  252.4 39.0 reduce-scatter.2
  353.7 58.0 all-gather.7
  428.5 40.2 reduce-scatter.4
  533.3 127.6 all-reduce.2
  663.4 79.5 all-reduce.4
